TPU v7x, 32 devices: a whole 2x2x4 slice. The times are simulated.
32 devices in a mesh: groups: 2 (over y), ex: 8 (over z, x), wid: 2 (over core).
Axes of the slice: x: 2, y: 2, z: 4, core: 2. Of those that a mesh axis runs over, the one named last changes fastest.
Arguments:
- train_sketch: bfloat16 [2048, 65536], P(('groups', 'ex'), 'wid'), parts along dimension 0, may hold values from -6 to 6
- query_sketch: bfloat16 [512, 65536], P(('groups', 'ex'), 'wid'), parts along dimension 0, may hold values from -6 to 6
- sign_bits: int32 [65536], P('wid'), may hold values from 0 to 1
- column_order: int32 [8192], replicated, may hold values from 0 to 8191, each once
- pair_blocks: int32 [32, 2], P('groups'), parts along dimension 0, may hold values from 0 to 15, as said below
Outputs:
- scores: float32 [2048, 32], P(('groups', 'ex')), parts along dimension 0
There are 2 independent parts, one for each index of `groups`. A program takes and returns all parts, laid end to end along the dimension named above; an argument that names none is the same for every part. Nothing has to cross between parts.
Inputs may be any that keep to these rules, and one draw needn't show every extreme that they name: `pair_blocks`: the 4 blocks named by the train blocks a 2 to (a + 1) * 2 - 1 for any a lie in distinct aligned runs of 2 query blocks.
All inputs are finite; a program needn't handle non-finite values.
Results may differ from a plain program's by a relative error of at most 0.0041.
Values may be sent and summed in bfloat16 or wider, within the bound.
A program may use at most 128 MiB of HBM per device.

v0:
```python
import math

import jax
import jax.numpy as jnp
from jax import lax
from jax.sharding import PartitionSpec as P

WIDTH = 65536
PROJ = 8192
HBLOCK = 512
TR_DEV = 128
TB_DEV = 2
QBLK = 16
TBLK = 64


def hadamard_table(order_size):
    positions = jnp.arange(order_size, dtype=jnp.int32)
    parity = jnp.zeros((order_size, order_size), jnp.int32)
    for bit_pos in range(order_size.bit_length() - 1):
        column_bit = jnp.right_shift(positions, bit_pos) & 1
        parity = parity + column_bit[:, None] * column_bit[None, :]
    return (1 - 2 * (parity % 2)).astype(jnp.bfloat16)


def project_rows(sketch_matrix, sign_vals, hadamard, column_order):
    row_count, local_width = sketch_matrix.shape
    flipped = (sketch_matrix * sign_vals[None, :]).reshape(row_count, local_width // HBLOCK, HBLOCK)
    rotated = jnp.einsum("nbh,hg->nbg", flipped, hadamard, preferred_element_type=jnp.float32)
    segments = rotated.reshape(row_count, local_width // PROJ // 2, 2, PROJ)
    even_sum = segments[:, :, 0, :].sum(axis=1)
    odd_sum = segments[:, :, 1, :].sum(axis=1)
    odd_moved = jnp.take(jnp.transpose(odd_sum), column_order, axis=0)
    folded = even_sum + jnp.transpose(odd_moved)
    return folded * (1.0 / math.sqrt(HBLOCK * (WIDTH // PROJ)))


def body(train_sketch, query_sketch, sign_bits, column_order, pair_blocks):
    hadamard = hadamard_table(HBLOCK)
    sign_vals = (2 * sign_bits - 1).astype(jnp.bfloat16)
    train_part = project_rows(train_sketch, sign_vals, hadamard, column_order)
    query_part = project_rows(query_sketch, sign_vals, hadamard, column_order)
    train_sum, query_sum = (
        lax.psum_scatter(train_part, "wid", scatter_dimension=1, tiled=True),
        lax.psum_scatter(query_part, "wid", scatter_dimension=1, tiled=True),
    )
    train_proj = train_sum.astype(jnp.bfloat16)
    query_proj = query_sum.astype(jnp.bfloat16)
    slot_count = pair_blocks.shape[1]
    device_pos = lax.axis_index("ex")
    local_pairs = lax.dynamic_slice_in_dim(pair_blocks, device_pos * TB_DEV, TB_DEV, 0)
    first_row = local_pairs * QBLK
    target_rows = first_row[:, :, None] + jnp.arange(QBLK, dtype=jnp.int32)[None, None, :]
    target_rows = target_rows.reshape(TB_DEV, slot_count * QBLK)
    segment = lax.all_gather(query_proj, "ex", axis=0, tiled=True)
    seg_rows = segment.shape[0]
    full_scores = lax.dot_general(
        train_proj, segment, (((1,), (1,)), ((), ())), preferred_element_type=jnp.float32
    )
    row_pos = jnp.arange(seg_rows, dtype=jnp.int32)
    placement = (target_rows[:, :, None] == row_pos[None, None, :]).astype(jnp.float32)
    block_scores = full_scores.reshape(TB_DEV, TBLK, seg_rows)
    added_tiles = jnp.einsum(
        "bxr,bcr->bxc",
        block_scores,
        placement,
        precision=lax.Precision.HIGHEST,
        preferred_element_type=jnp.float32,
    )
    partial_tiles = added_tiles.reshape(TR_DEV, slot_count * QBLK)
    scores = lax.psum(partial_tiles, "wid") * (1.0 / math.sqrt(PROJ))
    return scores


def solution(mesh):
    placed = (
        P(("groups", "ex"), "wid"),
        P(("groups", "ex"), "wid"),
        P("wid"),
        P(),
        P("groups", None),
    )
    return jax.shard_map(
        body, mesh=mesh, in_specs=placed, out_specs=P(("groups", "ex"), None), check_vma=False
    )
```

profile of v0, /device:TPU:0, one launch (start us, length us, event | category | flops | bytes accessed | tf_op | source)
XLA Modules:
  0.0 171.9 jit_solution(13792888885251499541)
XLA Ops:
  6.6 0.8 fusion.17
  7.3 0.8 compare_and_fusion
  8.1 0.9 add_convert_fusion
  9.0 1.9 %broadcast_multiply_fusion.1 = bf16[32,32768]{1,0:T(8,128)(2,1)S(1)} fusion(bf16[32,32768]{1,0:T(8,128)(2,1)} %param.6, bf16[32768]{0:T(1024)(128)(2,1)S(1)} %add_convert_fusion), kind=kLoop, calls=%fused_computation.21 | loop fusion | flops 1048576 | bytes 4259840 | tf_op jit(solution)/shard_map/mul | solution.py:28
  10.9 0.7 copy.27
  11.7 3.9 %fusion.12 = f32[32,64,512]{2,1,0:T(8,128)} fusion(bf16[32,64,512]{2,1,0:T(8,128)(2,1)S(1)} %bitcast.32, s32[512]{0:T(512)S(1)} %get-tuple-element.9, s32[512]{0:T(512)S(1)} %get-tuple-element.10, s32[512]{0:T(512)S(1)} %get-tuple-element.11, s32[512]{0:T(512)S(1)} %get-tuple-element.12, s32[512]{0:T(512)S(1)} %get-tuple-element.13, ...), kind=kOutput, calls=%fused_computation.25 | convolution fusion | flops 1081868288 | bytes 6309888 | tf_op jit(solution)/shard_map/nbh,hg->nbg/dot_general | solution.py:29
  15.6 6.6 %reshape.132 = f32[32,2,2,8192]{3,2,1,0:T(2,128)} reshape(f32[32,64,512]{2,1,0:T(8,128)} %fusion.12) | data formatting | bytes 8388608 | tf_op jit(solution)/shard_map/reshape | solution.py:30
  22.2 9.0 %slice_reduce_fusion.2 = (f32[32,8192]{1,0:T(8,128)S(1)}, f32[32,8192]{1,0:T(8,128)S(1)}) fusion(f32[32,2,2,8192]{3,2,1,0:T(2,128)} %reshape.132), kind=kLoop, calls=%fused_computation.10 | loop fusion | flops 524288 | bytes 6291456 | tf_op jit(solution)/shard_map/reduce_sum | solution.py:32
  31.2 2.6 %copy.21 = f32[32,8192]{0,1:T(8,128)} copy(f32[32,8192]{1,0:T(8,128)S(1)} %get-tuple-element.7) | data formatting | bytes 2097152 | tf_op jit(solution)/shard_map/reduce_sum | solution.py:32
  33.9 29.9 %gather_fusion.1 = f32[8192,32]{1,0:T(8,128)} fusion(f32[8192,32]{1,0:T(8,128)} %bitcast.27, s32[8192]{0:T(1024)S(1)} %fusion.17), kind=kCustom, calls=%fused_computation.1 | custom fusion | bytes 2129920 | tf_op jit(solution)/shard_map/jit(_take)/gather | solution.py:33
  63.8 2.8 %copy.22 = f32[8192,32]{0,1:T(8,128)S(1)} copy(f32[8192,32]{1,0:T(8,128)} %gather_fusion.1) | data formatting | bytes 2097152 | tf_op jit(solution)/shard_map/jit(_take)/gather | solution.py:33
  66.6 1.1 fusion.8
  67.8 7.9 %broadcast_multiply_fusion = bf16[128,32768]{1,0:T(8,128)(2,1)} fusion(bf16[128,32768]{1,0:T(8,128)(2,1)} %param.5, bf16[32768]{0:T(1024)(128)(2,1)S(1)} %add_convert_fusion), kind=kLoop, calls=%fused_computation.9 | loop fusion | flops 4194304 | bytes 16842752 | tf_op jit(solution)/shard_map/mul | solution.py:28
  75.7 3.4 %reduce-scatter.5.cloned.1.call-done = f32[32,4096]{1,0:T(8,128)} async-done(((f32[32,8192]{1,0:T(8,128)}), f32[32,4096]{1,0:T(8,128)}) %reduce-scatter.5.cloned.1.call-update) | async-done | bytes 524304 | tf_op jit(solution)/shard_map/reduce_scatter | solution.py:45
  79.1 1.8 %convert_element_type.18 = bf16[32,4096]{1,0:T(8,128)(2,1)} convert(f32[32,4096]{1,0:T(8,128)} %reduce-scatter.5.cloned.1.call-done) | non-fusion elementwise | flops 131072 | bytes 786432 | tf_op jit(solution)/shard_map/convert_element_type | solution.py:48
  80.9 0.2 reduce-scatter.3.cloned.1.call-start
  81.2 14.7 %fusion = f32[128,64,512]{0,2,1:T(8,128)} fusion(bf16[16,64,8,512]{3,2,1,0:T(8,128)(2,1)} %bitcast.30, s32[512]{0:T(512)S(1)} %get-tuple-element.9, s32[512]{0:T(512)S(1)} %get-tuple-element.10, s32[512]{0:T(512)S(1)} %get-tuple-element.11, s32[512]{0:T(512)S(1)} %get-tuple-element.12, s32[512]{0:T(512)S(1)} %get-tuple-element.13, ...), kind=kOutput, calls=%fused_computation.2 | convolution fusion | flops 4303093760 | bytes 25184256 | tf_op jit(solution)/shard_map/nbh,hg->nbg/dot_general | solution.py:29
  95.9 10.4 %slice_reduce_fusion = (f32[128,8192]{0,1:T(8,128)}, f32[128,8192]{0,1:T(8,128)}) fusion(f32[128,2,2,8192]{0,3,2,1:T(8,128)} %bitcast.29), kind=kLoop, calls=%fused_computation.5 | loop fusion | flops 2097152 | bytes 25165824 | tf_op jit(solution)/shard_map/reduce_sum | solution.py:32
  106.3 29.9 %gather_fusion = f32[8192,128]{1,0:T(8,128)} fusion(f32[8192,128]{1,0:T(8,128)} %bitcast.28, s32[8192]{0:T(1024)S(1)} %fusion.17), kind=kCustom, calls=%fused_computation | custom fusion | bytes 8421376 | tf_op jit(solution)/shard_map/jit(_take)/gather | solution.py:33
  136.2 8.3 %fusion.3 = f32[128,8192]{0,1:T(8,128)} fusion(f32[128,8192]{0,1:T(8,128)} %get-tuple-element.6, f32[8192,128]{1,0:T(8,128)} %gather_fusion, pred[8192]{0:T(1024)(128)(4,1)S(1)} %compare_and_fusion), kind=kLoop, calls=%fused_computation.8 | loop fusion | flops 3145728 | bytes 12591104 | tf_op jit(solution)/shard_map/mul | solution.py:35
  144.5 0.6 copy-done
  145.1 0.1 dynamic-slice_multiply_fusion
  145.2 0.1 copy.23
  145.3 0.1 add.113
  145.3 0.1 add.114
  145.4 0.1 add.116
  145.5 12.3 %reduce-scatter.3.cloned.1.call-done = f32[128,4096]{0,1:T(8,128)} async-done(((f32[128,8192]{0,1:T(8,128)}), f32[128,4096]{0,1:T(8,128)}) %reduce-scatter.3.cloned.1.call-update) | async-done | bytes 2097168 | tf_op jit(solution)/shard_map/reduce_scatter | solution.py:44
  157.8 3.0 %fusion.9 = f32[128,256]{1,0:T(8,128)S(1)} fusion(bf16[256,4096]{1,0:T(8,128)(2,1)} %all-gather.2.cloned.1.call-done, f32[128,4096]{0,1:T(8,128)} %reduce-scatter.3.cloned.1.call-done), kind=kOutput, calls=%fused_computation.22 | convolution fusion | flops 268959744 | bytes 4325376 | tf_op jit(solution)/shard_map/dot_general | solution.py:57
  160.9 0.2 fusion.15
  161.2 0.1 reshape.134
  161.2 3.5 %psum.7 = f32[128,32]{0,1:T(8,128)S(1)} all-reduce(f32[128,32]{0,1:T(8,128)S(1)} %reshape.134), channel_id=1, replica_groups=mesh['groups'=2,'ex'=8,'wid'=2] {'wid'}, use_global_device_ids=true, to_apply=%region_6.7 | all-reduce | flops 4096 | bytes 32768 | tf_op jit(solution)/shard_map/psum | solution.py:71
  164.7 0.6 broadcast_multiply_fusion.2
  (15 shorter events, 0.2 us)
Async XLA Ops:
  6.5 72.6 %reduce-scatter.5.cloned.1.call-start = ((), (), s32[]{:S(2)}) async-start(), calls=%async_computation.3 | async-start | bytes 1572864 | tf_op jit(solution)/shard_map/reduce_scatter | solution.py:45
  67.7 77.8 %all-gather.2.cloned.1.call-start = ((), (), s32[]{:S(2)}) async-start(), calls=%async_computation.4 | async-start | bytes 2359296 | tf_op jit(solution)/shard_map/all_gather | solution.py:55
  80.9 76.9 %reduce-scatter.3.cloned.1.call-start = ((), (), s32[]{:S(2)}) async-start(), calls=%async_computation.2 | async-start | bytes 6291456 | tf_op jit(solution)/shard_map/reduce_scatter | solution.py:44
  144.4 0.7 copy-start
Sparse Core Ops, SparseCore 0:
  67.8 11.2 reduce-scatter.4
  81.5 50.4 all-gather.1
  144.6 13.2 reduce-scatter.2
where the time goes:
time: 173 us; the launch traced here: 172 us
  local copies, waits for them, and re-layouts  73.6 us (43%)
  other arithmetic  43.6 us (25%)
  matrix products  21.9 us (13%)
  waiting for transfers between devices  15.8 us (9%)
  between operations  13.2 us (8%)
  blocking collectives  3.5 us (2%)
    gather x3, local copies, waits for them, and re-layouts, project_rows(): odd_moved = jnp.take(jnp.transpose(odd_sum), column_order, axis=0)  62.6 us
    reduce_sum x2, other arithmetic, project_rows(): odd_sum = segments[:, :, 1, :].sum(axis=1)  19.4 us
    dot_general x2, matrix products, project_rows(): jnp.einsum('nbh,hg->nbg', flipped, hadamard, preferred_element_type=jnp.f...  18.6 us
    reduce_scatter x1, waiting for transfers between devices, body(): lax.psum_scatter(train_part, 'wid', scatter_dimension=1, tiled=True)  12.3 us
    mul x2, other arithmetic, project_rows(): sketch_matrix * sign_vals[None, :]  9.81 us
    mul x2, other arithmetic, project_rows(): return folded * (1.0 / math.sqrt(HBLOCK * (WIDTH // PROJ)))  9.38 us
    reshape x1, local copies, waits for them, and re-layouts, project_rows(): segments = rotated.reshape(row_count, local_width // PROJ // 2, 2, PROJ)  6.58 us
    psum x1, blocking collectives, body(): scores = lax.psum(partial_tiles, 'wid') * (1.0 / math.sqrt(PROJ))  3.5 us
  transfers between devices with their start and end apart: 3, of which 2 were waited for; matrix products, arithmetic and copies ran while one was open for 42% of the time, Pallas kernels for 0%

commit v1 on v0

v1 whole, which is shorter than its diff:
```python
import functools
import math

import jax
import jax.numpy as jnp
import numpy as np
from jax import lax
from jax.experimental import pallas as pl
from jax.experimental.pallas import tpu as pltpu
from jax.sharding import PartitionSpec as P

WIDTH = 65536
PROJ = 8192
HBLOCK = 512
TB_DEV = 2
QBLK = 16
TBLK = 64
STEP = 1024
MESH = pl.DeviceIdType.MESH


def hadamard_table(order_size):
    table = np.ones((1, 1), np.float32)
    while table.shape[0] < order_size:
        table = np.block([[table, table], [table, -table]])
    return table.astype(jnp.bfloat16)


def fold_kernel(seg_count, half, *refs):
    order_ref, had_ref = refs[0], refs[1]
    train_refs = refs[2:2 + seg_count]
    query_refs = refs[2 + seg_count:2 + 2 * seg_count]
    sign_refs = refs[2 + 2 * seg_count:2 + 3 * seg_count]
    query_out, train_out, even_t, even_q, odd_t, odd_q = refs[2 + 3 * seg_count:]
    step = pl.program_id(0)
    train_rows = train_out.shape[1]
    query_rows = query_out.shape[1]
    hadamard = had_ref[...]
    for sub in range(STEP // HBLOCK):
        cols = pl.ds(sub * HBLOCK, HBLOCK)
        sums = [None, None]
        for seg in range(seg_count):
            signs = sign_refs[seg][:, cols]
            rows = jnp.concatenate([train_refs[seg][:, cols], query_refs[seg][:, cols]], axis=0)
            term = lax.dot_general(
                hadamard, rows * signs, (((1,), (1,)), ((), ())), preferred_element_type=jnp.float32
            )
            sums[seg % 2] = term if sums[seg % 2] is None else sums[seg % 2] + term
        place = pl.ds(pl.multiple_of(step * STEP + sub * HBLOCK, HBLOCK), HBLOCK)
        even_t[place, :] = sums[0][:, :train_rows]
        even_q[place, :query_rows] = sums[0][:, train_rows:]
        odd_t[place, :] = sums[1][:, :train_rows]
        odd_q[place, :query_rows] = sums[1][:, train_rows:]

    @pl.when(step == pl.num_programs(0) - 1)
    def _():
        @pl.loop(0, PROJ // 32)
        def _(group):
            first = pl.multiple_of(group * 32, 32)
            for part in range(4):
                start = pl.multiple_of(first + part * 8, 8)
                places = [order_ref[start + row] for row in range(8)]
                here = pl.ds(start, 8)
                even_t[here, :] += jnp.concatenate([odd_t[pl.ds(at, 1), :] for at in places], axis=0)
                even_q[here, :] += jnp.concatenate([odd_q[pl.ds(at, 1), :] for at in places], axis=0)

        for side in range(2):
            @pl.loop(0, half // HBLOCK)
            def _(block):
                cols = pl.ds(pl.multiple_of(block * HBLOCK, HBLOCK), HBLOCK)
                rows = pl.ds(pl.multiple_of(side * half + block * HBLOCK, HBLOCK), HBLOCK)
                train_out[side, :, cols] = even_t[rows, :].T
                query_out[side, :, cols] = even_q[rows, :].T[:query_rows, :]


def fold_rows(train_sketch, query_sketch, sign_vals, column_order, hadamard):
    train_rows, local_width = train_sketch.shape
    query_rows = query_sketch.shape[0]
    seg_count = local_width // PROJ
    half = PROJ // 2
    steps = PROJ // STEP

    def pieces(rows):
        return [
            pl.BlockSpec((rows, STEP), functools.partial(lambda seg, i: (0, seg * steps + i), seg))
            for seg in range(seg_count)
        ]

    return pl.pallas_call(
        functools.partial(fold_kernel, seg_count, half),
        grid=(steps,),
        out_shape=(
            jax.ShapeDtypeStruct((2, query_rows, half), jnp.float32),
            jax.ShapeDtypeStruct((2, train_rows, half), jnp.float32),
        ),
        in_specs=[
            pl.BlockSpec(memory_space=pltpu.SMEM),
            pl.BlockSpec((HBLOCK, HBLOCK), lambda i: (0, 0)),
            *pieces(train_rows),
            *pieces(query_rows),
            *pieces(1),
        ],
        out_specs=(
            pl.BlockSpec((2, query_rows, half), lambda i: (0, 0, 0)),
            pl.BlockSpec((2, train_rows, half), lambda i: (0, 0, 0)),
        ),
        scratch_shapes=[pltpu.VMEM((PROJ, 128), jnp.float32)] * 4,
        compiler_params=pltpu.CompilerParams(vmem_limit_bytes=48 * 1024 * 1024),
        name="fold_rows",
    )(
        column_order,
        hadamard,
        *[train_sketch] * seg_count,
        *[query_sketch] * seg_count,
        *[sign_vals.reshape(1, local_width)] * seg_count,
    )


def score_kernel(
    outer, inner, query_ref, train_ref, out_ref, query_got, train_got, segment, train_proj, part, part_got,
    wid_send, wid_recv, send_sem, recv_sem,
):
    wid = lax.axis_index("wid")
    other = 1 - wid
    pos = lax.axis_index("ex")
    row, col = pos // inner, lax.rem(pos, inner)
    query_rows = query_ref.shape[1]
    outer_peers = [lax.rem(row + d, outer) for d in range(1, outer)]
    inner_peers = [lax.rem(col + d, inner) for d in range(1, inner)]

    barrier = pltpu.get_barrier_semaphore()
    pl.semaphore_signal(barrier, inc=1, device_id={"wid": other}, device_id_type=MESH)
    for peer in outer_peers:
        pl.semaphore_signal(barrier, inc=1, device_id={"ex": peer * inner + col}, device_id_type=MESH)
    for peer in inner_peers:
        pl.semaphore_signal(barrier, inc=1, device_id={"ex": row * inner + peer}, device_id_type=MESH)
    pl.semaphore_wait(barrier, outer + inner - 1)

    def swap(source, target, index):
        return pltpu.make_async_remote_copy(
            src_ref=source, dst_ref=target, send_sem=wid_send.at[index], recv_sem=wid_recv.at[index],
            device_id={"wid": other}, device_id_type=MESH,
        )

    def slot_rows(slot):
        return segment.at[pl.ds(pl.multiple_of(slot * query_rows, query_rows), query_rows), :]

    def push(slot, target, index):
        return pltpu.make_async_remote_copy(
            src_ref=slot_rows(slot), dst_ref=slot_rows(slot), send_sem=send_sem.at[index],
            recv_sem=recv_sem.at[slot], device_id={"ex": target}, device_id_type=MESH,
        )

    scale = 1.0 / math.sqrt(HBLOCK * (WIDTH // PROJ))
    query_swap = swap(query_ref.at[other], query_got, 0)
    query_swap.start()
    train_swap = swap(train_ref.at[other], train_got, 1)
    query_swap.wait()
    own = pl.ds(pl.multiple_of(pos * query_rows, query_rows), query_rows)
    segment[own, :] = ((query_ref[wid] + query_got[...]) * scale).astype(jnp.bfloat16)
    sent = []

    def send(slot, target):
        copy = push(slot, target, len(sent))
        copy.start()
        sent.append(copy)

    for peer in outer_peers:
        send(pos, peer * inner + col)
    for peer in inner_peers:
        send(pos, row * inner + peer)
    train_swap.start()
    train_swap.wait()
    train_proj[...] = ((train_ref[wid] + train_got[...]) * scale).astype(jnp.bfloat16)
    for d in range(1, outer):
        slot = lax.rem(row + outer - d, outer) * inner + col
        push(slot, pos, 0).wait_recv()
        for peer in inner_peers:
            send(slot, row * inner + peer)
    for d in range(outer):
        for peer in inner_peers:
            push(lax.rem(row + outer - d, outer) * inner + peer, pos, 0).wait_recv()
    width = min(256, part.shape[1])
    for first in range(0, part.shape[1], width):
        part[:, pl.ds(first, width)] = lax.dot_general(
            train_proj[...], segment[pl.ds(first, width), :], (((1,), (1,)), ((), ())),
            preferred_element_type=jnp.float32,
        )
    part_swap = swap(part, part_got, 2)
    part_swap.start()
    part_swap.wait()
    out_ref[...] = (part[...] + part_got[...]) * (1.0 / math.sqrt(PROJ))
    for copy in sent:
        copy.wait_send()


def score_rows(query_part, train_part, ex_count):
    _, query_rows, half = query_part.shape
    train_rows = train_part.shape[1]
    outer = 4 if ex_count % 4 == 0 else 1
    inner = ex_count // outer
    width = ex_count * query_rows
    return pl.pallas_call(
        functools.partial(score_kernel, outer, inner),
        out_shape=jax.ShapeDtypeStruct((train_rows, width), jnp.float32),
        in_specs=[pl.BlockSpec(memory_space=pltpu.VMEM)] * 2,
        out_specs=pl.BlockSpec(memory_space=pltpu.VMEM),
        scratch_shapes=[
            pltpu.VMEM((query_rows, half), jnp.float32),
            pltpu.VMEM((train_rows, half), jnp.float32),
            pltpu.VMEM((width, half), jnp.bfloat16),
            pltpu.VMEM((train_rows, half), jnp.bfloat16),
            pltpu.VMEM((train_rows, width), jnp.float32),
            pltpu.VMEM((train_rows, width), jnp.float32),
            pltpu.SemaphoreType.DMA((3,)),
            pltpu.SemaphoreType.DMA((3,)),
            pltpu.SemaphoreType.DMA((outer - 1 + outer * (inner - 1),)),
            pltpu.SemaphoreType.DMA((ex_count,)),
        ],
        compiler_params=pltpu.CompilerParams(
            collective_id=0, has_side_effects=True, vmem_limit_bytes=48 * 1024 * 1024
        ),
        name="score_rows",
    )(query_part, train_part)


def body(ex_count, train_sketch, query_sketch, sign_bits, column_order, pair_blocks):
    hadamard = jnp.asarray(hadamard_table(HBLOCK))
    sign_vals = (2 * sign_bits - 1).astype(jnp.bfloat16)
    query_part, train_part = fold_rows(train_sketch, query_sketch, sign_vals, column_order, hadamard)
    slot_count = pair_blocks.shape[1]
    device_pos = lax.axis_index("ex")
    local_pairs = lax.dynamic_slice_in_dim(pair_blocks, device_pos * TB_DEV, TB_DEV, 0)
    target_rows = (local_pairs * QBLK)[:, :, None] + jnp.arange(QBLK, dtype=jnp.int32)[None, None, :]
    target_rows = target_rows.reshape(TB_DEV, slot_count * QBLK)
    full_scores = score_rows(query_part, train_part, ex_count)
    seg_rows = full_scores.shape[1]
    row_pos = jnp.arange(seg_rows, dtype=jnp.int32)
    placement = (target_rows[:, :, None] == row_pos[None, None, :]).astype(jnp.float32)
    scores = jnp.einsum(
        "bxr,bcr->bxc",
        full_scores.reshape(TB_DEV, TBLK, seg_rows),
        placement,
        precision=lax.Precision.HIGHEST,
        preferred_element_type=jnp.float32,
    )
    return scores.reshape(TB_DEV * TBLK, slot_count * QBLK)


def solution(mesh):
    placed = (
        P(("groups", "ex"), "wid"),
        P(("groups", "ex"), "wid"),
        P("wid"),
        P(),
        P("groups", None),
    )
    return jax.shard_map(
        functools.partial(body, mesh.shape["ex"]),
        mesh=mesh, in_specs=placed, out_specs=P(("groups", "ex"), None), check_vma=False,
    )
```

time: 173 us -> 80.3 us (0.46)
  the two profiles are of different devices: /device:TPU:0 before, /device:TPU:29 now
where the time goes in v1:
time: 80.3 us; the launch traced here: 80 us
  Pallas kernels  72 us (90%)
  local copies, waits for them, and re-layouts  6.72 us (8%)
  other arithmetic  1 us (1%)
    pallas_call x1, Pallas kernels, score_rows(): pl.pallas_call(functools.partial(score_kernel, outer, inner), out_shape=j...  44.1 us
    pallas_call x1, Pallas kernels, fold_rows(): pl.pallas_call(functools.partial(fold_kernel, seg_count, half), grid=(ste...  27.8 us
    unnamed x10, local copies, waits for them, and re-layouts  5.59 us

profile of v1, /device:TPU:29, one launch (start us, length us, event | category | flops | bytes accessed | tf_op | source)
XLA Modules:
  0.0 80.0 jit_solution(7444613651141705089)
XLA Ops:
  0.0 0.9 %add_convert_fusion = bf16[32768]{0:T(1024)(128)(2,1)S(1)} fusion(s32[32768]{0:T(1024)} %param.8), kind=kLoop, calls=%fused_computation | loop fusion | flops 98304 | bytes 196608 | tf_op jit(solution)/shard_map/convert_element_type | solution.py:229
  0.9 0.1 reshape.24.refs_10_.refs_11_.refs_12_.refs_13_
  1.0 0.0 copy-start
  1.0 1.6 %copy-done = bf16[32,32768]{1,0:T(8,128)(2,1)S(1)} copy-done((bf16[32,32768]{1,0:T(8,128)(2,1)S(1)}, bf16[32,32768]{1,0:T(8,128)(2,1)}, u32[]{:S(2)}) %copy-start) | copy-done | bytes 2097176
  2.6 0.0 copy-start.2
  2.6 1.0 %copy-done.2 = bf16[512,512]{1,0:T(8,128)(2,1)S(1)} copy-done((bf16[512,512]{1,0:T(8,128)(2,1)S(1)}, bf16[512,512]{1,0:T(8,128)(2,1)}, u32[]{:S(2)}) %copy-start.2) | copy-done | bytes 524312
  3.6 0.0 copy-start.3
  3.6 0.8 copy-done.3
  4.4 27.8 %fold_rows.1 = (f32[2,32,4096]{2,1,0:T(8,128)S(1)}, f32[2,128,4096]{2,1,0:T(8,128)}) custom-call(s32[8192]{0:T(1024)S(1)} %copy-done.3, bf16[512,512]{1,0:T(8,128)(2,1)S(1)} %copy-done.2, bf16[128,32768]{1,0:T(8,128)(2,1)} %refs_5_.1, bf16[128,32768]{1,0:T(8,128)(2,1)} %refs_5_.1, bf16[128,32768]{1,0:T(8,128)(2,1)} %refs_5_.1, bf16[128,32768]{1,0:T(8,128)(2,1)} %refs_5_.1, ...), custom_call_target="tpu_custom_call" | custom-call | tf_op jit(solution)/shard_map/fold_rows/pallas_call | solution.py:89
  32.2 0.0 copy-start.4
  32.2 0.0 copy-start.1
  32.2 2.2 %copy-done.1 = f32[2,128,4096]{2,1,0:T(8,128)S(1)} copy-done((f32[2,128,4096]{2,1,0:T(8,128)S(1)}, f32[2,128,4096]{2,1,0:T(8,128)}, u32[]{:S(2)}) %copy-start.1) | copy-done | bytes 4194328
  34.4 44.1 %score_rows.1 = f32[128,256]{1,0:T(8,128)S(1)} custom-call(f32[2,32,4096]{2,1,0:T(8,128)S(1)} %get-tuple-element.7.query_ref, f32[2,128,4096]{2,1,0:T(8,128)S(1)} %copy-done.1), custom_call_target="tpu_custom_call" | custom-call | tf_op jit(solution)/shard_map/score_rows/pallas_call | solution.py:203
  78.6 0.0 copy-done.4
  78.6 0.1 dynamic-slice_multiply_fusion
  78.7 0.1 copy.8
  78.8 0.1 add.28
  78.8 0.1 add.29
  78.9 0.1 add.31
  79.0 0.2 fusion
  79.3 0.7 reshape.26
  (3 shorter events, 0.0 us)
Async XLA Ops:
  1.0 1.6 %copy-start = (bf16[32,32768]{1,0:T(8,128)(2,1)S(1)}, bf16[32,32768]{1,0:T(8,128)(2,1)}, u32[]{:S(2)}) copy-start(bf16[32,32768]{1,0:T(8,128)(2,1)} %refs_9_.1) | copy-start | bytes 6291460
  2.6 1.0 %copy-start.2 = (bf16[512,512]{1,0:T(8,128)(2,1)S(1)}, bf16[512,512]{1,0:T(8,128)(2,1)}, u32[]{:S(2)}) copy-start(bf16[512,512]{1,0:T(8,128)(2,1)} %constant.19.clone.refs_1_) | copy-start | bytes 1572868
  3.6 0.8 copy-start.3
  32.2 46.4 %copy-start.4 = (s32[16,2]{0,1:T(2,128)S(1)}, s32[16,2]{0,1:T(2,128)}, u32[]{:S(2)}) copy-start(s32[16,2]{0,1:T(2,128)} %param.10) | copy-start | bytes 388
  32.2 2.2 %copy-start.1 = (f32[2,128,4096]{2,1,0:T(8,128)S(1)}, f32[2,128,4096]{2,1,0:T(8,128)}, u32[]{:S(2)}) copy-start(f32[2,128,4096]{2,1,0:T(8,128)} %get-tuple-element.8.train_ref) | copy-start | bytes 12582916

commit v2 on v0

v2 whole, which is shorter than its diff:
```python
import functools
import math

import jax
import jax.numpy as jnp
import numpy as np
from jax import lax
from jax.experimental import pallas as pl
from jax.experimental.pallas import tpu as pltpu
from jax.sharding import PartitionSpec as P

WIDTH = 65536
PROJ = 8192
HBLOCK = 512
TB_DEV = 2
QBLK = 16
TBLK = 64
CHUNK = 16
DOT_ROWS = 512
MESH = pl.DeviceIdType.MESH


def hadamard_table(order_size):
    table = np.ones((1, 1), np.float32)
    while table.shape[0] < order_size:
        table = np.block([[table, table], [table, -table]])
    return table.astype(jnp.bfloat16)


def rotate_group(group, rows, sketch, signs, hadamard, even_part, odd_part):
    half = PROJ // 2
    blocks = DOT_ROWS // rows
    for parity in range(2):
        total = None
        for seg in range(parity, sketch.shape[1] // PROJ, 2):
            pieces = []
            for block in range(blocks):
                start = pl.multiple_of(seg * PROJ + (group * blocks + block) * HBLOCK, HBLOCK)
                cols = pl.ds(start, HBLOCK)
                pieces.append(sketch[:, cols] * signs[:, cols])
            term = jnp.dot(
                jnp.concatenate(pieces, axis=0), hadamard[...], preferred_element_type=jnp.float32
            )
            total = term if total is None else total + term
        for block in range(blocks):
            start = (group * blocks + block) * HBLOCK
            value = total[block * rows:(block + 1) * rows, :]
            if parity == 0:
                side = start // half
                even_part[side, :, pl.ds(pl.multiple_of(start - side * half, HBLOCK), HBLOCK)] = value
            else:
                odd_part[:, pl.ds(pl.multiple_of(start, HBLOCK), HBLOCK)] = value


def turn_odd(rows, odd_part, odd_got, odd_rows):
    @pl.loop(0, PROJ // HBLOCK)
    def _(block):
        span = pl.ds(pl.multiple_of(block * HBLOCK, HBLOCK), HBLOCK)
        odd_rows[span, :rows] = (odd_part[:, span] + odd_got[:, span]).T


def move_rows(base, first, last, order, odd_rows, moved):
    @pl.loop(first // 32, last // 32)
    def _(group):
        for part in range(4):
            start = pl.multiple_of(group * 32 + part * 8, 8)
            places = [order[base + start + row] for row in range(8)]
            moved[pl.ds(start, 8), :] = jnp.concatenate([odd_rows[pl.ds(at, 1), :] for at in places], axis=0)


def fold_half(rows, wid, even_part, even_got, moved, target, target_row):
    scale = 1.0 / math.sqrt(HBLOCK * (WIDTH // PROJ))

    @pl.loop(0, PROJ // 2 // HBLOCK)
    def _(block):
        span = pl.ds(pl.multiple_of(block * HBLOCK, HBLOCK), HBLOCK)
        total = even_part[wid, :, span] + even_got[:, span] + moved[span, :].T[:rows, :]
        target[pl.ds(target_row, rows), span] = (total * scale).astype(jnp.bfloat16)


def score_kernel(
    outer, inner, order, hadamard, signs, query_hbm, train_hbm, out_ref,
    query_in, train_in, query_even, query_odd, query_even_got, query_odd_got,
    train_even, train_odd, train_even_got, train_odd_got, odd_rows, moved,
    segment, train_proj, part, part_got,
    load_sem, wid_send, wid_recv, up_sem, down_sem, inner_sem, recv_sem,
):
    wid = lax.axis_index("wid")
    other = 1 - wid
    pos = lax.axis_index("ex")
    row, col = pos // inner, lax.rem(pos, inner)
    query_rows, train_rows = query_in.shape[0], train_in.shape[0]
    half = PROJ // 2
    chunks = query_rows // CHUNK
    outer_peers = [lax.rem(row + d, outer) for d in range(1, outer)]
    inner_peers = [lax.rem(col + d, inner) for d in range(1, inner)]

    load_query = pltpu.make_async_copy(query_hbm, query_in, load_sem.at[0])
    load_train = pltpu.make_async_copy(train_hbm, train_in, load_sem.at[1])
    load_query.start()
    load_train.start()
    barrier = pltpu.get_barrier_semaphore()
    pl.semaphore_signal(barrier, inc=1, device_id={"wid": other}, device_id_type=MESH)
    for peer in outer_peers:
        pl.semaphore_signal(barrier, inc=1, device_id={"ex": peer * inner + col}, device_id_type=MESH)
    for peer in inner_peers:
        pl.semaphore_signal(barrier, inc=1, device_id={"ex": row * inner + peer}, device_id_type=MESH)

    def swap(source, target, index):
        return pltpu.make_async_remote_copy(
            src_ref=source, dst_ref=target, send_sem=wid_send.at[index], recv_sem=wid_recv.at[index],
            device_id={"wid": other}, device_id_type=MESH,
        )

    def push(slot, chunk, target, sem):
        rows = pl.ds(pl.multiple_of(slot * query_rows + chunk * CHUNK, CHUNK), CHUNK)
        return pltpu.make_async_remote_copy(
            src_ref=segment.at[rows, :], dst_ref=segment.at[rows, :], send_sem=sem,
            recv_sem=recv_sem.at[slot * chunks + chunk], device_id={"ex": target}, device_id_type=MESH,
        )

    def up(step, chunk):
        return push((row - step) * inner + col, chunk, (row + 1) * inner + col, up_sem.at[step * chunks + chunk])

    def down(step, chunk):
        return push((row + step) * inner + col, chunk, (row - 1) * inner + col, down_sem.at[step * chunks + chunk])

    def across(from_row, step, chunk):
        return [
            push(
                from_row * inner + col, chunk, row * inner + peer,
                inner_sem.at[((step + outer - 1) * chunks + chunk) * (inner - 1) + index],
            )
            for index, peer in enumerate(inner_peers)
        ]

    def forward(step, chunk, act):
        @pl.when(row >= step)
        def _():
            if act is run:
                push((row - step) * inner + col, chunk, pos, up_sem.at[0]).wait_recv()

            @pl.when(row < outer - 1)
            def _():
                act(up(step, chunk))

            for copy in across(row - step, -step, chunk):
                act(copy)

        @pl.when(row + step < outer)
        def _():
            if act is run:
                push((row + step) * inner + col, chunk, pos, up_sem.at[0]).wait_recv()

            @pl.when(row > 0)
            def _():
                act(down(step, chunk))

            for copy in across(row + step, step, chunk):
                act(copy)

    def own(chunk, act):
        @pl.when(row < outer - 1)
        def _():
            act(up(0, chunk))

        @pl.when(row > 0)
        def _():
            act(down(0, chunk))

        for copy in across(row, 0, chunk):
            act(copy)

    def run(copy):
        copy.start()

    def finish(copy):
        copy.wait_send()

    load_query.wait()
    for group in range(PROJ // HBLOCK * query_rows // DOT_ROWS):
        rotate_group(group, query_rows, query_in, signs, hadamard, query_even, query_odd)
    pl.semaphore_wait(barrier, outer + inner - 1)
    odd_swap = swap(query_odd, query_odd_got, 0)
    even_swap = swap(query_even.at[other], query_even_got, 1)
    odd_swap.start()
    even_swap.start()
    odd_swap.wait()
    turn_odd(query_rows, query_odd, query_odd_got, odd_rows)
    move_rows(wid * half, 0, half, order, odd_rows, moved)
    even_swap.wait()
    own_row = pl.multiple_of(pos * query_rows, query_rows)
    fold_half(query_rows, wid, query_even, query_even_got, moved, segment, own_row)
    for chunk in range(chunks):
        own(chunk, run)

    train_odd_swap = swap(train_odd, train_odd_got, 2)
    train_even_swap = swap(train_even.at[other], train_even_got, 3)
    groups = PROJ // HBLOCK * train_rows // DOT_ROWS

    def rotate_span(first, last):
        @pl.loop(first, last)
        def _(group):
            rotate_group(group, train_rows, train_in, signs, hadamard, train_even, train_odd)

    def first_part():
        load_train.wait()
        rotate_span(0, groups // 2)

    def second_part():
        rotate_span(groups // 2, groups)
        train_odd_swap.start()
        train_even_swap.start()

    def third_part():
        train_odd_swap.wait()
        turn_odd(train_rows, train_odd, train_odd_got, odd_rows)

    def fourth_part():
        move_rows(wid * half, 0, half // 2, order, odd_rows, moved)

    def fifth_part():
        move_rows(wid * half, half // 2, half, order, odd_rows, moved)

    def sixth_part():
        train_even_swap.wait()
        fold_half(train_rows, wid, train_even, train_even_got, moved, train_proj, 0)

    work = [first_part, second_part, third_part, fourth_part, fifth_part, sixth_part]
    for step in range(1, outer):
        for chunk in range(chunks):
            if work:
                work.pop(0)()
            forward(step, chunk, run)
    for piece in work:
        piece()
    for d in range(outer):
        for peer in inner_peers:
            for chunk in range(chunks):
                push(lax.rem(row + d, outer) * inner + peer, chunk, pos, up_sem.at[0]).wait_recv()
    width = min(256, part.shape[1])
    for first in range(0, part.shape[1], width):
        part[:, pl.ds(first, width)] = lax.dot_general(
            train_proj[...], segment[pl.ds(first, width), :], (((1,), (1,)), ((), ())),
            preferred_element_type=jnp.float32,
        )
    part_swap = swap(part, part_got, 4)
    part_swap.start()
    for chunk in range(chunks):
        own(chunk, finish)
        for step in range(1, outer):
            forward(step, chunk, finish)
    part_swap.wait()
    out_ref[...] = (part[...] + part_got[...]) * (1.0 / math.sqrt(PROJ))


def score_rows(train_sketch, query_sketch, sign_vals, column_order, hadamard, ex_count):
    train_rows, local_width = train_sketch.shape
    query_rows = query_sketch.shape[0]
    half = PROJ // 2
    outer = 4 if ex_count % 4 == 0 else 1
    inner = ex_count // outer
    width = ex_count * query_rows
    chunks = query_rows // CHUNK

    def swapped(rows):
        return [
            pltpu.VMEM((2, rows, half), jnp.float32),
            pltpu.VMEM((rows, PROJ), jnp.float32),
            pltpu.VMEM((rows, half), jnp.float32),
            pltpu.VMEM((rows, PROJ), jnp.float32),
        ]

    return pl.pallas_call(
        functools.partial(score_kernel, outer, inner),
        out_shape=jax.ShapeDtypeStruct((train_rows, width), jnp.float32),
        in_specs=[
            pl.BlockSpec(memory_space=pltpu.SMEM),
            pl.BlockSpec(memory_space=pltpu.VMEM),
            pl.BlockSpec(memory_space=pltpu.VMEM),
            pl.BlockSpec(memory_space=pl.ANY),
            pl.BlockSpec(memory_space=pl.ANY),
        ],
        out_specs=pl.BlockSpec(memory_space=pltpu.VMEM),
        scratch_shapes=[
            pltpu.VMEM((query_rows, local_width), jnp.bfloat16),
            pltpu.VMEM((train_rows, local_width), jnp.bfloat16),
            *swapped(query_rows),
            *swapped(train_rows),
            pltpu.VMEM((PROJ, 128), jnp.float32),
            pltpu.VMEM((half, 128), jnp.float32),
            pltpu.VMEM((width, half), jnp.bfloat16),
            pltpu.VMEM((train_rows, half), jnp.bfloat16),
            pltpu.VMEM((train_rows, width), jnp.float32),
            pltpu.VMEM((train_rows, width), jnp.float32),
            pltpu.SemaphoreType.DMA((2,)),
            pltpu.SemaphoreType.DMA((5,)),
            pltpu.SemaphoreType.DMA((5,)),
            pltpu.SemaphoreType.DMA((outer * chunks,)),
            pltpu.SemaphoreType.DMA((outer * chunks,)),
            pltpu.SemaphoreType.DMA((max(1, (2 * outer - 1) * chunks * (inner - 1)),)),
            pltpu.SemaphoreType.DMA((ex_count * chunks,)),
        ],
        compiler_params=pltpu.CompilerParams(
            collective_id=0, has_side_effects=True, vmem_limit_bytes=60 * 1024 * 1024
        ),
        name="score_rows",
    )(column_order, hadamard, sign_vals.reshape(1, local_width), query_sketch, train_sketch)


def body(ex_count, train_sketch, query_sketch, sign_bits, column_order, pair_blocks):
    hadamard = jnp.asarray(hadamard_table(HBLOCK))
    sign_vals = (2 * sign_bits - 1).astype(jnp.bfloat16)
    slot_count = pair_blocks.shape[1]
    device_pos = lax.axis_index("ex")
    local_pairs = lax.dynamic_slice_in_dim(pair_blocks, device_pos * TB_DEV, TB_DEV, 0)
    target_rows = (local_pairs * QBLK)[:, :, None] + jnp.arange(QBLK, dtype=jnp.int32)[None, None, :]
    target_rows = target_rows.reshape(TB_DEV, slot_count * QBLK)
    full_scores = score_rows(train_sketch, query_sketch, sign_vals, column_order, hadamard, ex_count)
    seg_rows = full_scores.shape[1]
    row_pos = jnp.arange(seg_rows, dtype=jnp.int32)
    placement = (target_rows[:, :, None] == row_pos[None, None, :]).astype(jnp.float32)
    scores = jnp.einsum(
        "bxr,bcr->bxc",
        full_scores.reshape(TB_DEV, TBLK, seg_rows),
        placement,
        precision=lax.Precision.HIGHEST,
        preferred_element_type=jnp.float32,
    )
    return scores.reshape(TB_DEV * TBLK, slot_count * QBLK)


def solution(mesh):
    placed = (
        P(("groups", "ex"), "wid"),
        P(("groups", "ex"), "wid"),
        P("wid"),
        P(),
        P("groups", None),
    )
    return jax.shard_map(
        functools.partial(body, mesh.shape["ex"]),
        mesh=mesh, in_specs=placed, out_specs=P(("groups", "ex"), None), check_vma=False,
    )
```

time: 173 us -> 53.3 us (0.31)
  local copies, waits for them, and re-layouts: 73.6 us -> 1.79 us
  Pallas kernels: 0 us -> 49.2 us
  other arithmetic: 43.6 us -> 1.02 us
  matrix products: 21.9 us -> 1.13 us
  waiting for transfers between devices: 15.8 us -> 0 us
  between operations: 13.2 us -> 0.04 us
  blocking collectives: 3.5 us -> 0 us
    gather x3 -> x0, local copies, waits for them, and re-layouts: 62.6 us -> none  [project_rows(): odd_moved = jnp.take(jnp.transpose(odd_sum), column_order, axis=0)]
    pallas_call x0 -> x1, Pallas kernels: none -> 49.2 us  [score_rows(): pl.pallas_call(functools.partial(score_kernel, outer, inner), out_shape=j...]
    dot_general x4 -> x1, matrix products: 21.9 us -> 1.13 us  [body(): jnp.einsum('bxr,bcr->bxc', full_scores.reshape(TB_DEV, TBLK, seg_rows), p...]
    mul x6 -> x1, other arithmetic: 19.9 us -> 0.07 us  [body(): local_pairs * QBLK]
    reduce_sum x2 -> x0, other arithmetic: 19.4 us -> none  [project_rows(): odd_sum = segments[:, :, 1, :].sum(axis=1)]
    reduce_scatter x2 -> x0, waiting for transfers between devices: 15.7 us -> none  [the longest x1 12.3 us: body(): lax.psum_scatter(train_part, 'wid', scatter_dimension=1, tiled=True)]
    reshape x2, local copies, waits for them, and re-layouts: 6.66 us -> 1.41 us  [the longest x1 0.72 us: score_rows(): sign_vals.reshape(1, local_width)]
    psum x1 -> x0, blocking collectives: 3.5 us -> none  [body(): scores = lax.psum(partial_tiles, 'wid') * (1.0 / math.sqrt(PROJ))]
  transfers between devices with their start and end apart: 3 -> 0, of which waited for: 2 -> 0; matrix products, arithmetic and copies ran while one was open for 42% -> 0% of each run, Pallas kernels for 0% -> 0%
where the time goes in v2:
time: 53.3 us; the launch traced here: 53.1 us
  Pallas kernels  49.2 us (92%)
  local copies, waits for them, and re-layouts  1.79 us (3%)
  matrix products  1.13 us (2%)
  other arithmetic  1.02 us (2%)
    pallas_call x1, Pallas kernels, score_rows(): pl.pallas_call(functools.partial(score_kernel, outer, inner), out_shape=j...  49.2 us
    dot_general x1, matrix products, body(): jnp.einsum('bxr,bcr->bxc', full_scores.reshape(TB_DEV, TBLK, seg_rows), p...  1.13 us

profile of v2, /device:TPU:0, one launch (start us, length us, event | category | flops | bytes accessed | tf_op | source)
XLA Modules:
  0.0 53.1 jit_solution(3981527009000169882)
XLA Ops:
  0.0 0.0 copy-start
  0.0 0.9 %add_convert_fusion = bf16[32768]{0:T(1024)(128)(2,1)S(1)} fusion(s32[32768]{0:T(1024)} %param.8), kind=kLoop, calls=%fused_computation | loop fusion | flops 98304 | bytes 196608 | tf_op jit(solution)/shard_map/convert_element_type | solution.py:313
  0.9 0.7 %reshape.24.signs = bf16[1,32768]{1,0:T(2,128)(2,1)} reshape(bf16[32768]{0:T(1024)(128)(2,1)S(1)} %add_convert_fusion) | data formatting | bytes 131072 | tf_op jit(solution)/shard_map/reshape | solution.py:308
  1.7 49.2 %score_rows.1 = f32[128,256]{1,0:T(8,128)} custom-call(s32[8192]{0:T(1024)} %order.1, bf16[512,512]{1,0:T(8,128)(2,1)} %constant.19.clone.hadamard, bf16[1,32768]{1,0:T(2,128)(2,1)} %reshape.24.signs, bf16[32,32768]{1,0:T(8,128)(2,1)} %query_hbm.1, bf16[128,32768]{1,0:T(8,128)(2,1)} %train_hbm.1), custom_call_target="tpu_custom_call" | custom-call | tf_op jit(solution)/shard_map/score_rows/pallas_call | solution.py:274
  50.8 0.0 copy-done
  50.8 0.1 dynamic-slice_multiply_fusion
  50.9 0.1 copy.8
  51.0 0.1 add.28
  51.1 0.1 add.29
  51.2 0.1 add.31
  51.3 1.1 %fusion = f32[2,64,32]{1,2,0:T(8,128)S(1)} fusion(f32[2,64,256]{2,1,0:T(8,128)} %bitcast.4, s32[2,32]{1,0:T(2,128)S(1)} %broadcast_add_fusion), kind=kOutput, calls=%fused_computation.2 | convolution fusion | flops 12599296 | bytes 147712 | tf_op jit(solution)/shard_map/bxr,bcr->bxc/dot_general | solution.py:323
  52.4 0.7 %reshape.26 = f32[128,32]{0,1:T(8,128)} reshape(f32[2,64,32]{1,0,2:T(2,128)S(1)} %copy.9) | data formatting | bytes 32768 | tf_op jit(solution)/shard_map/reshape | solution.py:330
  (3 shorter events, 0.0 us)
Async XLA Ops:
  0.0 50.8 %copy-start = (s32[16,2]{0,1:T(2,128)S(1)}, s32[16,2]{0,1:T(2,128)}, u32[]{:S(2)}) copy-start(s32[16,2]{0,1:T(2,128)} %param.10) | copy-start | bytes 388

commit v3 on v2

v3 whole, which is shorter than its diff:
```python
import functools
import math

import jax
import jax.numpy as jnp
import numpy as np
from jax import lax
from jax.experimental import pallas as pl
from jax.experimental.pallas import tpu as pltpu
from jax.sharding import PartitionSpec as P

WIDTH = 65536
PROJ = 8192
HBLOCK = 512
QBLK = 16
TBLK = 64
CHUNKS = 4
DOT_ROWS = 512
MESH = pl.DeviceIdType.MESH


def hadamard_table(order_size):
    table = np.ones((1, 1), np.float32)
    while table.shape[0] < order_size:
        table = np.block([[table, table], [table, -table]])
    return table.astype(jnp.bfloat16)


def rotate_group(group, rows, sketch, signs, hadamard, even_part, odd_part, even_out=None, odd_out=None):
    half = PROJ // 2
    blocks = DOT_ROWS // rows
    for parity in range(2):
        total = None
        for seg in range(parity, sketch.shape[1] // PROJ, 2):
            pieces = []
            for block in range(blocks):
                start = pl.multiple_of(seg * PROJ + (group * blocks + block) * HBLOCK, HBLOCK)
                cols = pl.ds(start, HBLOCK)
                flip = (2 * signs[:, cols] - 1).astype(jnp.float32).astype(jnp.bfloat16)
                pieces.append(sketch[:, cols] * flip)
            term = jnp.dot(
                jnp.concatenate(pieces, axis=0), hadamard[...], preferred_element_type=jnp.float32
            )
            total = term if total is None else total + term
        for block in range(blocks):
            start = (group * blocks + block) * HBLOCK
            value = total[block * rows:(block + 1) * rows, :].astype(even_part.dtype)
            if parity == 0:
                side = start // half
                span = pl.ds(pl.multiple_of(start - side * half, HBLOCK), HBLOCK)
                even_part[side, :, span] = value
                if even_out is not None:
                    even_out[side, :, span] = value.astype(even_out.dtype)
            else:
                span = pl.ds(pl.multiple_of(start, HBLOCK), HBLOCK)
                odd_part[:, span] = value
                if odd_out is not None:
                    odd_out[:, span] = value.astype(odd_out.dtype)


def turn_odd(rows, odd_part, odd_got, odd_rows):
    @pl.loop(0, PROJ // HBLOCK)
    def _(block):
        span = pl.ds(pl.multiple_of(block * HBLOCK, HBLOCK), HBLOCK)
        odd_rows[span, :rows] = (odd_part[:, span] + odd_got[:, span]).T


def move_rows(base, first, last, order, odd_rows, moved):
    @pl.loop(first // 32, last // 32)
    def _(group):
        for part in range(4):
            start = pl.multiple_of(group * 32 + part * 8, 8)
            places = [order[base + start + row] for row in range(8)]
            moved[pl.ds(start, 8), :] = jnp.concatenate([odd_rows[pl.ds(at, 1), :] for at in places], axis=0)


def fold_half(first, last, rows, wid, even_part, even_got, moved, target, target_row):
    scale = 1.0 / math.sqrt(HBLOCK * (WIDTH // PROJ))

    @pl.loop(first // HBLOCK, last // HBLOCK)
    def _(block):
        span = pl.ds(pl.multiple_of(block * HBLOCK, HBLOCK), HBLOCK)
        total = even_part[wid, :, span] + even_got[:, span] + moved[span, :].T[:rows, :]
        target[pl.ds(target_row, rows), span] = (total * scale).astype(jnp.bfloat16)


def score_kernel(
    outer, inner, order, pairs, hadamard, signs, query_hbm, train_hbm, out_ref,
    query_in, train_in, query_even_out, query_odd_out, query_even, query_odd, query_even_got, query_odd_got,
    train_even, train_odd, train_even_got, train_odd_got, odd_rows, moved,
    segment, train_proj, part, picked, picked_got,
    load_sem, wid_send, wid_recv, up_sem, down_sem, inner_sem, recv_sem,
):
    wid = lax.axis_index("wid")
    other = 1 - wid
    pos = lax.axis_index("ex")
    row, col = pos // inner, lax.rem(pos, inner)
    query_rows, train_rows = query_in.shape[0], train_in.shape[0]
    half = PROJ // 2
    chunks = CHUNKS
    piece = half // chunks
    outer_peers = [lax.rem(row + d, outer) for d in range(1, outer)]
    inner_peers = [lax.rem(col + d, inner) for d in range(1, inner)]

    load_query = pltpu.make_async_copy(query_hbm, query_in, load_sem.at[0])
    load_train = pltpu.make_async_copy(train_hbm, train_in, load_sem.at[1])
    load_query.start()
    barrier = pltpu.get_barrier_semaphore()
    pl.semaphore_signal(barrier, inc=1, device_id={"wid": other}, device_id_type=MESH)
    for peer in outer_peers:
        pl.semaphore_signal(barrier, inc=1, device_id={"ex": peer * inner + col}, device_id_type=MESH)
    for peer in inner_peers:
        pl.semaphore_signal(barrier, inc=1, device_id={"ex": row * inner + peer}, device_id_type=MESH)

    def swap(source, target, index):
        return pltpu.make_async_remote_copy(
            src_ref=source, dst_ref=target, send_sem=wid_send.at[index], recv_sem=wid_recv.at[index],
            device_id={"wid": other}, device_id_type=MESH,
        )

    def push(slot, chunk, target, sem):
        rows = pl.ds(pl.multiple_of(slot * query_rows, query_rows), query_rows)
        span = pl.ds(chunk * piece, piece)
        return pltpu.make_async_remote_copy(
            src_ref=segment.at[rows, span], dst_ref=segment.at[rows, span], send_sem=sem,
            recv_sem=recv_sem.at[slot * chunks + chunk], device_id={"ex": target}, device_id_type=MESH,
        )

    def up(step, chunk):
        return push((row - step) * inner + col, chunk, (row + 1) * inner + col, up_sem.at[step * chunks + chunk])

    def down(step, chunk):
        return push((row + step) * inner + col, chunk, (row - 1) * inner + col, down_sem.at[step * chunks + chunk])

    def across(from_row, step, chunk):
        return [
            push(
                from_row * inner + col, chunk, row * inner + peer,
                inner_sem.at[((step + outer - 1) * chunks + chunk) * (inner - 1) + index],
            )
            for index, peer in enumerate(inner_peers)
        ]

    def forward(step, chunk, act):
        @pl.when(row >= step)
        def _():
            if act is run:
                push((row - step) * inner + col, chunk, pos, up_sem.at[0]).wait_recv()

            @pl.when(row < outer - 1)
            def _():
                act(up(step, chunk))

            for copy in across(row - step, -step, chunk):
                act(copy)

        @pl.when(row + step < outer)
        def _():
            if act is run:
                push((row + step) * inner + col, chunk, pos, up_sem.at[0]).wait_recv()

            @pl.when(row > 0)
            def _():
                act(down(step, chunk))

            for copy in across(row + step, step, chunk):
                act(copy)

    def own(chunk, act):
        @pl.when(row < outer - 1)
        def _():
            act(up(0, chunk))

        @pl.when(row > 0)
        def _():
            act(down(0, chunk))

        for copy in across(row, 0, chunk):
            act(copy)

    def run(copy):
        copy.start()

    def finish(copy):
        copy.wait_send()

    load_query.wait()
    load_train.start()
    for group in range(PROJ // HBLOCK * query_rows // DOT_ROWS):
        rotate_group(group, query_rows, query_in, signs, hadamard, query_even, query_odd, query_even_out, query_odd_out)
    pl.semaphore_wait(barrier, outer + inner - 1)
    odd_swap = swap(query_odd_out, query_odd_got, 0)
    even_swap = swap(query_even_out.at[other], query_even_got, 1)
    odd_swap.start()
    even_swap.start()
    odd_swap.wait()
    turn_odd(query_rows, query_odd, query_odd_got, odd_rows)
    even_swap.wait()
    own_row = pl.multiple_of(pos * query_rows, query_rows)
    for chunk in range(chunks):
        first, last = chunk * piece, (chunk + 1) * piece
        move_rows(wid * half, first, last, order, odd_rows, moved)
        fold_half(first, last, query_rows, wid, query_even, query_even_got, moved, segment, own_row)
        own(chunk, run)

    groups = PROJ // HBLOCK * train_rows // DOT_ROWS
    span_of = PROJ // groups
    odd_spans = [pl.ds(group * span_of, span_of) for group in range(groups)]
    train_odd_swaps = [
        swap(train_odd.at[:, span], train_odd_got.at[:, span], 3 + group) for group, span in enumerate(odd_spans)
    ]
    train_even_swap = swap(train_even.at[other], train_even_got, 3 + groups)

    def rotate_part(group):
        if group == 0:
            load_train.wait()
        rotate_group(group, train_rows, train_in, signs, hadamard, train_even, train_odd)
        train_odd_swaps[group].start()
        if group == groups - 1:
            train_even_swap.start()

    def turn_part():
        for copy in train_odd_swaps:
            copy.wait()
        turn_odd(train_rows, train_odd, train_odd_got, odd_rows)

    def move_part(index):
        move_rows(wid * half, index * piece, (index + 1) * piece, order, odd_rows, moved)

    def fold_part():
        train_even_swap.wait()
        fold_half(0, half, train_rows, wid, train_even, train_even_got, moved, train_proj, 0)

    work = [functools.partial(rotate_part, group) for group in range(groups)]
    work += [lambda: None, turn_part]
    work += [functools.partial(move_part, index) for index in range(chunks)]
    work += [fold_part]
    for step in range(1, outer):
        for chunk in range(chunks):
            if work:
                work.pop(0)()
            forward(step, chunk, run)
    for task in work:
        task()
    for d in range(outer):
        for peer in inner_peers:
            for chunk in range(chunks):
                push(lax.rem(row + d, outer) * inner + peer, chunk, pos, up_sem.at[0]).wait_recv()
    width = min(256, segment.shape[0])
    for first in range(0, segment.shape[0], width):
        tile = lax.dot_general(
            segment[pl.ds(first, width), :], train_proj[...], (((1,), (1,)), ((), ())),
            preferred_element_type=jnp.float32,
        )
        part[pl.ds(first // QBLK, width // QBLK)] = tile.reshape(width // QBLK, QBLK, train_rows)
    lanes = lax.broadcasted_iota(jnp.int32, (QBLK, train_rows), 1)
    for slot in range(pairs.shape[1]):
        tile = None
        for block in range(train_rows // TBLK):
            rows = part[pairs[pos * (train_rows // TBLK) + block, slot]]
            tile = rows if tile is None else jnp.where(lanes >= block * TBLK, rows, tile)
        picked[pl.ds(slot * QBLK, QBLK), :] = tile
    picked_swap = swap(picked, picked_got, 2)
    picked_swap.start()
    for chunk in range(chunks):
        own(chunk, finish)
        for step in range(1, outer):
            forward(step, chunk, finish)
    picked_swap.wait()
    out_ref[...] = ((picked[...] + picked_got[...]) * (1.0 / math.sqrt(PROJ)))


def score_rows(train_sketch, query_sketch, sign_bits, column_order, pair_blocks, hadamard, ex_count):
    train_rows, local_width = train_sketch.shape
    query_rows = query_sketch.shape[0]
    half = PROJ // 2
    outer = 4 if ex_count % 4 == 0 else 1
    inner = ex_count // outer
    width = ex_count * query_rows
    chunks = CHUNKS
    out_width = pair_blocks.shape[1] * QBLK
    groups = PROJ // HBLOCK * train_rows // DOT_ROWS

    def swapped(rows, kind):
        return [
            pltpu.VMEM((2, rows, half), jnp.float32),
            pltpu.VMEM((rows, PROJ), jnp.float32),
            pltpu.VMEM((rows, half), kind),
            pltpu.VMEM((rows, PROJ), kind),
        ]

    return pl.pallas_call(
        functools.partial(score_kernel, outer, inner),
        out_shape=jax.ShapeDtypeStruct((out_width, train_rows), jnp.float32),
        in_specs=[
            pl.BlockSpec(memory_space=pltpu.SMEM),
            pl.BlockSpec(memory_space=pltpu.SMEM),
            pl.BlockSpec(memory_space=pltpu.VMEM),
            pl.BlockSpec(memory_space=pltpu.VMEM),
            pl.BlockSpec(memory_space=pl.ANY),
            pl.BlockSpec(memory_space=pl.ANY),
        ],
        out_specs=pl.BlockSpec(memory_space=pltpu.VMEM),
        scratch_shapes=[
            pltpu.VMEM((query_rows, local_width), jnp.bfloat16),
            pltpu.VMEM((train_rows, local_width), jnp.bfloat16),
            pltpu.VMEM((2, query_rows, half), jnp.bfloat16),
            pltpu.VMEM((query_rows, PROJ), jnp.bfloat16),
            *swapped(query_rows, jnp.bfloat16),
            *swapped(train_rows, jnp.float32),
            pltpu.VMEM((PROJ, 128), jnp.float32),
            pltpu.VMEM((half, 128), jnp.float32),
            pltpu.VMEM((width, half), jnp.bfloat16),
            pltpu.VMEM((train_rows, half), jnp.bfloat16),
            pltpu.VMEM((width // QBLK, QBLK, train_rows), jnp.float32),
            pltpu.VMEM((out_width, train_rows), jnp.float32),
            pltpu.VMEM((out_width, train_rows), jnp.float32),
            pltpu.SemaphoreType.DMA((2,)),
            pltpu.SemaphoreType.DMA((4 + groups,)),
            pltpu.SemaphoreType.DMA((4 + groups,)),
            pltpu.SemaphoreType.DMA((outer * chunks,)),
            pltpu.SemaphoreType.DMA((outer * chunks,)),
            pltpu.SemaphoreType.DMA((max(1, (2 * outer - 1) * chunks * (inner - 1)),)),
            pltpu.SemaphoreType.DMA((ex_count * chunks,)),
        ],
        compiler_params=pltpu.CompilerParams(
            collective_id=0, has_side_effects=True, vmem_limit_bytes=60 * 1024 * 1024
        ),
        name="score_rows",
    )(column_order, pair_blocks, hadamard, sign_bits.reshape(1, local_width), query_sketch, train_sketch)


def body(ex_count, train_sketch, query_sketch, sign_bits, column_order, pair_blocks):
    hadamard = jnp.asarray(hadamard_table(HBLOCK))
    return score_rows(train_sketch, query_sketch, sign_bits, column_order, pair_blocks, hadamard, ex_count).T


def solution(mesh):
    placed = (
        P(("groups", "ex"), "wid"),
        P(("groups", "ex"), "wid"),
        P("wid"),
        P(),
        P("groups", None),
    )
    return jax.shard_map(
        functools.partial(body, mesh.shape["ex"]),
        mesh=mesh, in_specs=placed, out_specs=P(("groups", "ex"), None), check_vma=False,
    )
```

time: 53.3 us -> 44.6 us (0.84)
  Pallas kernels: 49.2 us -> 41.6 us
  matrix products: 1.13 us -> 0 us
  other arithmetic: 1.02 us -> 0 us
  local copies, waits for them, and re-layouts: 1.79 us -> 2.68 us
    pallas_call x1, Pallas kernels: 49.2 us -> 41.6 us  [score_rows(): pl.pallas_call(functools.partial(score_kernel, outer, inner), out_shape=j...]
    unnamed x2, local copies, waits for them, and re-layouts: 0.01 us -> 2.68 us
    reshape x2 -> x0, local copies, waits for them, and re-layouts: 1.41 us -> none  [the longest x1 0.72 us: score_rows(): sign_vals.reshape(1, local_width)]
    dot_general x1 -> x0, matrix products: 1.13 us -> none  [body(): jnp.einsum('bxr,bcr->bxc', full_scores.reshape(TB_DEV, TBLK, seg_rows), p...]
    convert_element_type x1 -> x0, other arithmetic: 0.94 us -> none  [body(): sign_vals = (2 * sign_bits - 1).astype(jnp.bfloat16)]
where the time goes in v3:
time: 44.6 us; the launch traced here: 44.3 us
  Pallas kernels  41.6 us (93%)
  local copies, waits for them, and re-layouts  2.68 us (6%)
    pallas_call x1, Pallas kernels, score_rows(): pl.pallas_call(functools.partial(score_kernel, outer, inner), out_shape=j...  41.6 us
    unnamed x2, local copies, waits for them, and re-layouts  2.68 us

profile of v3, /device:TPU:0, one launch (start us, length us, event | category | flops | bytes accessed | tf_op | source)
XLA Modules:
  0.0 44.3 jit_solution(7580824767148297541)
XLA Ops:
  0.0 1.4 %copy.7.pairs = s32[16,2]{1,0:T(8,128)} copy(s32[16,2]{0,1:T(2,128)} %param.10) | data formatting | bytes 256 | tf_op args[4]
  1.4 41.6 %score_rows.1 = f32[32,128]{1,0:T(8,128)} custom-call(s32[8192]{0:T(1024)} %order.1, s32[16,2]{1,0:T(8,128)} %copy.7.pairs, bf16[512,512]{1,0:T(8,128)(2,1)} %constant.2.clone.hadamard, s32[1,32768]{1,0:T(1,128)} %bitcast.2, bf16[32,32768]{1,0:T(8,128)(2,1)} %query_hbm.1, bf16[128,32768]{1,0:T(8,128)(2,1)} %train_hbm.1), custom_call_target="tpu_custom_call" | custom-call | tf_op jit(solution)/shard_map/score_rows/pallas_call | solution.py:292
  43.0 1.3 %copy.9 = f32[128,32]{0,1:T(8,128)} copy(f32[128,32]{0,1:T(8,128)} %bitcast.3) | data formatting | bytes 32768

commit v4 on v3

--- a/solution.py
+++ b/solution.py
@@ -89,7 +89,7 @@
     query_in, train_in, query_even_out, query_odd_out, query_even, query_odd, query_even_got, query_odd_got,
     train_even, train_odd, train_even_got, train_odd_got, odd_rows, moved,
     segment, train_proj, part, picked, picked_got,
-    load_sem, wid_send, wid_recv, up_sem, down_sem, inner_sem, recv_sem,
+    load_sem, wid_send, wid_recv, up_sem, down_sem, relay_sem, inner_sem, recv_sem,
 ):
     wid = lax.axis_index("wid")
     other = 1 - wid
@@ -101,6 +101,7 @@
     piece = half // chunks
     outer_peers = [lax.rem(row + d, outer) for d in range(1, outer)]
     inner_peers = [lax.rem(col + d, inner) for d in range(1, inner)]
+    shared = chunks // 2 if inner == 2 and outer == 4 else 0
 
     load_query = pltpu.make_async_copy(query_hbm, query_in, load_sem.at[0])
     load_train = pltpu.make_async_copy(train_hbm, train_in, load_sem.at[1])
@@ -151,8 +152,10 @@
             def _():
                 act(up(step, chunk))
 
-            for copy in across(row - step, -step, chunk):
-                act(copy)
+            @pl.when((row > step) if chunk < shared else (row >= step))
+            def _():
+                for copy in across(row - step, -step, chunk):
+                    act(copy)
 
         @pl.when(row + step < outer)
         def _():
@@ -163,8 +166,31 @@
             def _():
                 act(down(step, chunk))
 
-            for copy in across(row + step, step, chunk):
-                act(copy)
+            @pl.when((row + step < outer - 1) if chunk < shared else (row + step < outer))
+            def _():
+                for copy in across(row + step, step, chunk):
+                    act(copy)
+
+    def relay(step, chunk, act):
+        @pl.when(row == step)
+        def _():
+            slot = inner_peers[0]
+            if act is run:
+                push(slot, chunk, pos, up_sem.at[0]).wait_recv()
+
+            @pl.when(row < outer - 1)
+            def _():
+                act(push(slot, chunk, (row + 1) * inner + col, relay_sem.at[chunk]))
+
+        @pl.when(row + step == outer - 1)
+        def _():
+            slot = (outer - 1) * inner + inner_peers[0]
+            if act is run:
+                push(slot, chunk, pos, up_sem.at[0]).wait_recv()
+
+            @pl.when(row > 0)
+            def _():
+                act(push(slot, chunk, (row - 1) * inner + col, relay_sem.at[chunks + chunk]))
 
     def own(chunk, act):
         @pl.when(row < outer - 1)
@@ -235,17 +261,22 @@
     work += [lambda: None, turn_part]
     work += [functools.partial(move_part, index) for index in range(chunks)]
     work += [fold_part]
+    work.pop(0)()
+    for chunk in range(shared):
+        relay(0, chunk, run)
     for step in range(1, outer):
         for chunk in range(chunks):
             if work:
                 work.pop(0)()
             forward(step, chunk, run)
+        for chunk in range(shared):
+            relay(step, chunk, run)
     for task in work:
         task()
-    for d in range(outer):
+    for from_row in range(outer):
         for peer in inner_peers:
-            for chunk in range(chunks):
-                push(lax.rem(row + d, outer) * inner + peer, chunk, pos, up_sem.at[0]).wait_recv()
+            for chunk in range(shared if from_row in (0, outer - 1) else 0, chunks):
+                push(from_row * inner + peer, chunk, pos, up_sem.at[0]).wait_recv()
     width = min(256, segment.shape[0])
     for first in range(0, segment.shape[0], width):
         tile = lax.dot_general(
@@ -254,10 +285,10 @@
         )
         part[pl.ds(first // QBLK, width // QBLK)] = tile.reshape(width // QBLK, QBLK, train_rows)
     lanes = lax.broadcasted_iota(jnp.int32, (QBLK, train_rows), 1)
-    for slot in range(pairs.shape[1]):
+    for slot in range(pairs.shape[0]):
         tile = None
         for block in range(train_rows // TBLK):
-            rows = part[pairs[pos * (train_rows // TBLK) + block, slot]]
+            rows = part[pairs[slot, pos * (train_rows // TBLK) + block]]
             tile = rows if tile is None else jnp.where(lanes >= block * TBLK, rows, tile)
         picked[pl.ds(slot * QBLK, QBLK), :] = tile
     picked_swap = swap(picked, picked_got, 2)
@@ -266,6 +297,9 @@
         own(chunk, finish)
         for step in range(1, outer):
             forward(step, chunk, finish)
+    for step in range(outer):
+        for chunk in range(shared):
+            relay(step, chunk, finish)
     picked_swap.wait()
     out_ref[...] = ((picked[...] + picked_got[...]) * (1.0 / math.sqrt(PROJ)))
 
@@ -320,6 +354,7 @@
             pltpu.SemaphoreType.DMA((4 + groups,)),
             pltpu.SemaphoreType.DMA((outer * chunks,)),
             pltpu.SemaphoreType.DMA((outer * chunks,)),
+            pltpu.SemaphoreType.DMA((2 * chunks,)),
             pltpu.SemaphoreType.DMA((max(1, (2 * outer - 1) * chunks * (inner - 1)),)),
             pltpu.SemaphoreType.DMA((ex_count * chunks,)),
         ],
@@ -327,7 +362,7 @@
             collective_id=0, has_side_effects=True, vmem_limit_bytes=60 * 1024 * 1024
         ),
         name="score_rows",
-    )(column_order, pair_blocks, hadamard, sign_bits.reshape(1, local_width), query_sketch, train_sketch)
+    )(column_order, pair_blocks.T, hadamard, sign_bits.reshape(1, local_width), query_sketch, train_sketch)
 
 
 def body(ex_count, train_sketch, query_sketch, sign_bits, column_order, pair_blocks):

time: 44.6 us -> 42.8 us (0.960)
  local copies, waits for them, and re-layouts: 2.68 us -> 1.32 us
    unnamed x2 -> x1, local copies, waits for them, and re-layouts: 2.68 us -> 1.32 us
where the time goes in v4:
time: 42.8 us; the launch traced here: 42.6 us
  Pallas kernels  41.3 us (96%)
  local copies, waits for them, and re-layouts  1.32 us (3%)
    pallas_call x1, Pallas kernels, score_rows(): pl.pallas_call(functools.partial(score_kernel, outer, inner), out_shape=j...  41.3 us
    unnamed x1, local copies, waits for them, and re-layouts  1.32 us

profile of v4, /device:TPU:0, one launch (start us, length us, event | category | flops | bytes accessed | tf_op | source)
XLA Modules:
  0.0 42.6 jit_solution(16184939195963573797)
XLA Ops:
  0.0 41.3 %score_rows.1 = f32[32,128]{1,0:T(8,128)} custom-call(s32[8192]{0:T(1024)} %order.1, s32[2,16]{1,0:T(2,128)} %bitcast.5, bf16[512,512]{1,0:T(8,128)(2,1)} %constant.2.clone.hadamard, s32[1,32768]{1,0:T(1,128)} %bitcast.3, bf16[32,32768]{1,0:T(8,128)(2,1)} %query_hbm.1, bf16[128,32768]{1,0:T(8,128)(2,1)} %train_hbm.1), custom_call_target="tpu_custom_call" | custom-call | tf_op jit(solution)/shard_map/score_rows/pallas_call | solution.py:326
  41.3 1.3 %copy.8 = f32[128,32]{0,1:T(8,128)} copy(f32[128,32]{0,1:T(8,128)} %bitcast.4) | data formatting | bytes 32768

commit v5 on v4

--- a/solution.py
+++ b/solution.py
@@ -26,10 +26,10 @@
     return table.astype(jnp.bfloat16)
 
 
-def rotate_group(group, rows, sketch, signs, hadamard, even_part, odd_part, even_out=None, odd_out=None):
+def rotate_group(group, rows, sketch, signs, hadamard, even_part, odd_part, even_out=None, odd_out=None, parities=(0, 1)):
     half = PROJ // 2
     blocks = DOT_ROWS // rows
-    for parity in range(2):
+    for parity in parities:
         total = None
         for seg in range(parity, sketch.shape[1] // PROJ, 2):
             pieces = []
@@ -212,12 +212,20 @@
 
     load_query.wait()
     load_train.start()
-    for group in range(PROJ // HBLOCK * query_rows // DOT_ROWS):
-        rotate_group(group, query_rows, query_in, signs, hadamard, query_even, query_odd, query_even_out, query_odd_out)
-    pl.semaphore_wait(barrier, outer + inner - 1)
     odd_swap = swap(query_odd_out, query_odd_got, 0)
     even_swap = swap(query_even_out.at[other], query_even_got, 1)
+
+    def rotate_query(parity):
+        for group in range(PROJ // HBLOCK * query_rows // DOT_ROWS):
+            rotate_group(
+                group, query_rows, query_in, signs, hadamard, query_even, query_odd, query_even_out, query_odd_out,
+                (parity,),
+            )
+
+    rotate_query(1)
+    pl.semaphore_wait(barrier, outer + inner - 1)
     odd_swap.start()
+    rotate_query(0)
     even_swap.start()
     odd_swap.wait()
     turn_odd(query_rows, query_odd, query_odd_got, odd_rows)

time: 42.8 us -> 42.3 us (0.988)
  Pallas kernels: 41.3 us -> 40.7 us
    pallas_call x1, Pallas kernels: 41.3 us -> 40.7 us  [score_rows(): pl.pallas_call(functools.partial(score_kernel, outer, inner), out_shape=j...]
where the time goes in v5:
time: 42.3 us; the launch traced here: 42.1 us
  Pallas kernels  40.7 us (96%)
  local copies, waits for them, and re-layouts  1.32 us (3%)
    pallas_call x1, Pallas kernels, score_rows(): pl.pallas_call(functools.partial(score_kernel, outer, inner), out_shape=j...  40.7 us
    unnamed x1, local copies, waits for them, and re-layouts  1.32 us

profile of v5, /device:TPU:0, one launch (start us, length us, event | category | flops | bytes accessed | tf_op | source)
XLA Modules:
  0.0 42.1 jit_solution(5022376622751273866)
XLA Ops:
  0.0 40.7 %score_rows.1 = f32[32,128]{1,0:T(8,128)} custom-call(s32[8192]{0:T(1024)} %order.1, s32[2,16]{1,0:T(2,128)} %bitcast.5, bf16[512,512]{1,0:T(8,128)(2,1)} %constant.2.clone.hadamard, s32[1,32768]{1,0:T(1,128)} %bitcast.3, bf16[32,32768]{1,0:T(8,128)(2,1)} %query_hbm.1, bf16[128,32768]{1,0:T(8,128)(2,1)} %train_hbm.1), custom_call_target="tpu_custom_call" | custom-call | tf_op jit(solution)/shard_map/score_rows/pallas_call | solution.py:334
  40.7 1.3 %copy.8 = f32[128,32]{0,1:T(8,128)} copy(f32[128,32]{0,1:T(8,128)} %bitcast.4) | data formatting | bytes 32768
